TPU v7x, 256 devices: a whole 4x4x8 slice. The times are simulated.
256 devices in a mesh: fsdp: 2 (over core), ctx: 128 (over z, x, y).
Axes of the slice: x: 4, y: 4, z: 8, core: 2. Of those that a mesh axis runs over, the one named last changes fastest.
Arguments:
- tokens: bfloat16 [2, 65536, 2048], P('fsdp', 'ctx'), may hold values from -6 to 6
- w_qkv: bfloat16 [2048, 3, 1024], P(None, None, 'fsdp'), may hold values from -0.125 to 0.125
- w_out: bfloat16 [1024, 2048], P('fsdp'), may hold values from -0.1875 to 0.1875
- gain: float32 [1024], replicated, may hold values from 0.1 to 1.9
Outputs:
- mixed: bfloat16 [2, 65536, 2048], P('fsdp', 'ctx')
All inputs are finite; a program needn't handle non-finite values.
Results may differ from a plain program's by a relative error of at most 0.007.
Values may be sent and summed in bfloat16 or wider, within the bound.
A program may use at most 192 MiB of HBM per device.

v0:
```python
import jax
import jax.numpy as jnp
from jax import lax
from jax.sharding import PartitionSpec as P

HD = 128


def prefix_2(value, axis, join, neutral):
    count, mine = (lax.axis_size(axis), lax.axis_index(axis))
    pieces = lax.all_gather(value, axis)
    running = jnp.full_like(value, 0) + jnp.asarray(neutral, value.dtype)

    def lap(position, running):
        longer = join(running, pieces[position])
        return jnp.where(position < mine, longer, running)

    return lax.fori_loop(0, count - 1, lap, running)


def project(rows, weight):
    mixed = jnp.einsum("btd,dgc->btgc", rows, weight, preferred_element_type=jnp.float32)
    return jax.nn.silu(mixed).astype(jnp.bfloat16)


def local_scores(query, key_rows, value_rows):
    length = query.shape[1]
    row_block = min(512, length)
    tok_idx = lax.broadcasted_iota(jnp.int32, (row_block, row_block), 0) + 0
    src_idx = lax.broadcasted_iota(jnp.int32, (row_block, row_block), 1)
    causal = tok_idx >= src_idx
    scores = jnp.einsum("bthe,bshe->bhts", query, key_rows, preferred_element_type=jnp.float32)
    scores = jnp.where(causal[None, None], scores, 0.0).astype(jnp.bfloat16)
    pieces = jnp.einsum("bhts,bshf->bthf", scores, value_rows, preferred_element_type=jnp.float32)
    return pieces


def attend(qkv, gain_cols):
    batch, length, three, cols = qkv.shape
    heads = cols // HD
    query = qkv[:, :, 0].reshape(batch, length, heads, HD)
    key_rows = qkv[:, :, 1].reshape(batch, length, heads, HD)
    value_rows = qkv[:, :, 2].reshape(batch, length, heads, HD)
    kv_block = jnp.einsum(
        "bthe,bthf->bhef", key_rows, value_rows, preferred_element_type=jnp.float32
    )
    prefix = prefix_2(kv_block, "ctx", jnp.add, jnp.zeros_like(kv_block))
    inter = jnp.einsum(
        "bthe,bhef->bthf", query.astype(jnp.float32), prefix, precision=lax.Precision.HIGHEST
    )
    intra = local_scores(query, key_rows, value_rows)
    total = inter + intra
    normed = (
        total
        * lax.rsqrt(jnp.mean(total * total, axis=-1, keepdims=True) + 1e-06)
        * gain_cols.reshape(heads, HD)
    )
    return normed.astype(jnp.bfloat16).reshape(batch, length, cols)


def body(tokens, w_qkv, w_out, gain):
    qkv = project(tokens, lax.all_gather(w_qkv, "fsdp", axis=2, tiled=True))
    normed = attend(qkv, gain)
    mixed = jnp.einsum(
        "btc,cd->btd",
        normed,
        lax.all_gather(w_out, "fsdp", axis=0, tiled=True),
        preferred_element_type=jnp.float32,
    )
    return mixed.astype(jnp.bfloat16)


def solution(mesh):
    in_specs = (P("fsdp", "ctx", None), P(None, None, "fsdp"), P("fsdp", None), P())
    out_specs = P("fsdp", "ctx", None)
    return jax.shard_map(body, mesh=mesh, in_specs=in_specs, out_specs=out_specs, check_vma=False)
```

profile of v0, /device:TPU:224, one launch (start us, length us, event | category | flops | bytes accessed | tf_op | source)
XLA Modules:
  0.0 574.2 jit_solution(1753249526962559987)
XLA Ops:
  7.3 32.6 %all-gather.5.cloned.1.call-done = bf16[2048,3,1024]{2,0,1:T(8,128)(2,1)} async-done(((bf16[2048,3,512]{2,0,1:T(8,128)(2,1)}), bf16[2048,3,1024]{2,0,1:T(8,128)(2,1)}) %all-gather.5.cloned.1.call-update) | async-done | bytes 12582928 | tf_op jit(solution)/shard_map/all_gather | solution.py:62
  39.9 10.3 %fusion.10 = bf16[1,512,3,1024]{3,1,2,0:T(8,128)(2,1)S(1)} fusion(bf16[2048,3,1024]{2,0,1:T(8,128)(2,1)} %all-gather.5.cloned.1.call-done, bf16[1,512,2048]{2,1,0:T(8,128)(2,1)S(1)} %copy-done), kind=kOutput, calls=%fused_computation.15 | convolution fusion | flops 6450315264 | bytes 17825792 | tf_op jit(solution)/shard_map/btd,dgc->btgc/dot_general | solution.py:22
  50.2 1.7 slice_bitcast_fusion
  51.9 1.5 copy.19
  53.4 2.7 copy.18
  56.1 2.5 fusion.18
  59.5 2.5 copy.20
  61.9 5.7 fusion
  67.6 331.3 %all-gather.9.cloned.1.call-done = f32[1024,128,128]{2,1,0:T(8,128)} async-done(((f32[8,128,128]{2,1,0:T(8,128)}), f32[1024,128,128]{2,1,0:T(8,128)}) %all-gather.9.cloned.1.call-update) | async-done | bytes 67108880 | tf_op jit(solution)/shard_map/all_gather | solution.py:11
  398.9 159.3 %while.14 = (s32[]{:T(128)}, f32[1,8,128,128]{3,2,1,0:T(8,128)S(1)}, s32[]{:T(128)}, f32[128,1,8,128,128]{4,3,2,1,0:T(8,128)}, s32[]{:T(128)}, /*index=5*/s32[]{:T(128)}) while((s32[]{:T(128)}, f32[1,8,128,128]{3,2,1,0:T(8,128)S(1)}, s32[]{:T(128)}, f32[128,1,8,128,128]{4,3,2,1,0:T(8,128)}, s32[]{:T(128)}, ...), condition=%wide.region_1.2_spmd.clone, body=%wide.region_0.1_spmd.clone.sunk | while | flops 393220 | bytes 1572957 | solution.py:18
  400.2 1.2 add_select_fusion.2
  401.4 1.2 add_select_fusion.2
  402.7 1.2 add_select_fusion.2
  403.9 1.2 add_select_fusion.2
  405.2 1.2 add_select_fusion.2
  406.4 1.2 add_select_fusion.2
  407.7 1.2 add_select_fusion.2
  408.9 1.2 add_select_fusion.2
  410.2 1.3 add_select_fusion.2
  411.5 1.3 add_select_fusion.2
  412.8 1.3 add_select_fusion.2
  414.1 1.4 add_select_fusion.2
  415.5 1.4 add_select_fusion.2
  416.9 1.2 add_select_fusion.2
  418.2 1.2 add_select_fusion.2
  419.4 1.2 add_select_fusion.2
  420.7 1.2 add_select_fusion.2
  421.9 1.2 add_select_fusion.2
  423.2 1.2 add_select_fusion.2
  424.4 1.2 add_select_fusion.2
  425.7 1.2 add_select_fusion.2
  426.9 1.2 add_select_fusion.2
  428.2 1.2 add_select_fusion.2
  429.4 1.2 add_select_fusion.2
  430.7 1.2 add_select_fusion.2
  431.9 1.2 add_select_fusion.2
  433.2 1.2 add_select_fusion.2
  434.4 1.2 add_select_fusion.2
  435.7 1.2 add_select_fusion.2
  436.9 1.2 add_select_fusion.2
  438.2 1.2 add_select_fusion.2
  439.4 1.2 add_select_fusion.2
  440.7 1.2 add_select_fusion.2
  441.9 1.2 add_select_fusion.2
  443.2 1.2 add_select_fusion.2
  444.4 1.2 add_select_fusion.2
  445.7 1.2 add_select_fusion.2
  446.9 1.2 add_select_fusion.2
  448.2 1.2 add_select_fusion.2
  449.4 1.2 add_select_fusion.2
  450.7 1.2 add_select_fusion.2
  452.0 1.2 add_select_fusion.2
  453.2 1.2 add_select_fusion.2
  462.0 1.2 add_select_fusion.2
  475.7 1.2 add_select_fusion.2
  485.7 1.2 add_select_fusion.2
  499.5 1.2 add_select_fusion.2
  509.5 1.2 add_select_fusion.2
  523.3 1.2 add_select_fusion.2
  533.3 1.2 add_select_fusion.2
  547.0 1.2 add_select_fusion.2
  557.0 1.2 add_select_fusion.2
  558.3 3.1 fusion.6
  561.8 5.9 %fusion.5 = bf16[1,512,2048]{2,1,0:T(8,128)(2,1)} fusion(bf16[512,1024]{0,1:T(8,128)(2,1)S(1)} %bitcast.56, bf16[1024,2048]{1,0:T(8,128)(2,1)} %all-gather.7.cloned.1.call-done), kind=kOutput, calls=%fused_computation.8 | convolution fusion | flops 2148532224 | bytes 7340032 | tf_op jit(solution)/shard_map/btc,cd->btd/dot_general | solution.py:64
  (92 shorter events, 93.9 us)
Async XLA Ops:
  6.5 33.3 %copy-start = (bf16[1,512,2048]{2,1,0:T(8,128)(2,1)S(1)}, bf16[1,512,2048]{2,1,0:T(8,128)(2,1)}, u32[]{:S(2)}) copy-start(bf16[1,512,2048]{2,1,0:T(8,128)(2,1)} %param.6) | copy-start | bytes 6291460
  6.5 33.3 %all-gather.5.cloned.1.call-start = ((), (), s32[]{:S(2)}) async-start(), calls=%async_computation | async-start | bytes 18874368 | tf_op jit(solution)/shard_map/all_gather | solution.py:62
  7.3 391.7 %all-gather.9.cloned.1.call-start = ((), (), s32[]{:S(2)}) async-start(), calls=%async_computation.2 | async-start | bytes 67633152 | tf_op jit(solution)/shard_map/all_gather | solution.py:11
  53.4 5.9 %copy-start.1 = (bf16[1,512,1,1024]{1,3,2,0:T(8,128)(2,1)}, bf16[1,512,1,1024]{1,3,2,0:T(8,128)(2,1)S(1)}, u32[]{:S(2)}) copy-start(bf16[1,512,1,1024]{1,3,2,0:T(8,128)(2,1)S(1)} %copy.19) | copy-start | bytes 3145732
  58.6 503.2 %all-gather.7.cloned.1.call-start = ((), (), s32[]{:S(2)}) async-start(), calls=%async_computation.1 | async-start | bytes 6291456 | tf_op jit(solution)/shard_map/all_gather | solution.py:67
  558.3 3.1 copy-start.2
Sparse Core Ops, SparseCore 0:
  9.2 30.6 all-gather.4
  58.7 340.1 all-gather.8
  400.7 18.0 all-gather.6
where the time goes:
time: 585 us; the launch traced here: 574 us
  waiting for transfers between devices  365 us (62%)
  other arithmetic  157 us (27%)
  matrix products  27.5 us (5%)
  between operations  13.2 us (2%)
  local copies, waits for them, and re-layouts  8.39 us (1%)
    all_gather x1, waiting for transfers between devices, prefix_2(): pieces = lax.all_gather(value, axis)  331 us
    select_n x127, other arithmetic, lap(): return jnp.where(position < mine, longer, running)  156 us
    all_gather x1, waiting for transfers between devices, body(): qkv = project(tokens, lax.all_gather(w_qkv, 'fsdp', axis=2, tiled=True))  32.6 us
  transfers between devices with their start and end apart: 3, of which 2 were waited for; matrix products, arithmetic and copies ran while one was open for 29% of the time, Pallas kernels for 0%

commit v1 on v0

v1 whole, which is shorter than its diff:
```python
import jax
import jax.numpy as jnp
from jax import lax
from jax.experimental import pallas as pl
from jax.experimental.pallas import tpu as pltpu
from jax.sharding import PartitionSpec as P

HD = 128
T = 512
D = 2048
NH = 4
HC = NH * HD
PLANE = 16
NZ = 8
SL = HC // PLANE
F32 = jnp.float32
BF16 = jnp.bfloat16
MESH = pl.DeviceIdType.MESH


def silu(v):
    half = 0.5 * v
    return half + half * jnp.tanh(half)


def remote(src, dst, send, recv, device):
    return pltpu.make_async_remote_copy(
        src_ref=src, dst_ref=dst, send_sem=send, recv_sem=recv, device_id=device, device_id_type=MESH
    )


def kernel(
    x_hbm, w_hbm, wo_hbm, gain_ref, out_hbm,
    x_own, x_oth, w, wo_own, wo_oth,
    qkv_a, qkv_s, qkv_r,
    kv_a, kv_b, r1a, r1b, t2a, t2b, r2a, r2b, o3a, o3b, pfa, pfb,
    y_a, y_b, n_a, n_b, acc, out_v,
    ld_sem, st_sem, ps_sem, pr_sem, s1_sem, q1_sem, s2_sem, q2_sem, s3_sem, q3_sem,
):
    f = lax.axis_index("fsdp")
    c = lax.axis_index("ctx")
    z = c // PLANE
    p = lax.rem(c, PLANE)
    base = z * PLANE
    g = 1 - f

    def chip(k):
        return lax.rem(p + k, PLANE)

    barrier = pltpu.get_barrier_semaphore()
    for k in range(PLANE):
        pl.semaphore_signal(barrier, inc=1, device_id=(g, base + chip(k)), device_id_type=MESH)
        if k:
            pl.semaphore_signal(barrier, inc=1, device_id=(f, base + chip(k)), device_id_type=MESH)
    for k in range(1, NZ):
        pl.semaphore_signal(
            barrier, inc=1, device_id=(f, lax.rem(z + k, NZ) * PLANE + p), device_id_type=MESH
        )

    loads = [pltpu.make_async_copy(x_hbm.at[0], x_own, ld_sem.at[0])]
    for n, which in enumerate((1, 2, 0)):
        loads.append(pltpu.make_async_copy(w_hbm.at[which], w.at[which], ld_sem.at[1 + n]))
    loads.append(pltpu.make_async_copy(wo_hbm, wo_own, ld_sem.at[4]))
    for copy in loads:
        copy.start()

    pl.semaphore_wait(barrier, 2 * PLANE - 1 + NZ - 1)

    partner = (g, c)
    send_x = remote(x_hbm.at[0], x_oth, ps_sem.at[0], pr_sem.at[0], partner)
    send_wo = remote(wo_hbm, wo_oth, ps_sem.at[1], pr_sem.at[1], partner)
    send_k = remote(
        qkv_s.at[:, pl.ds(HC, 2 * HC)], qkv_r.at[:, pl.ds(HC, 2 * HC)], ps_sem.at[2], pr_sem.at[2], partner
    )
    send_q = remote(qkv_s.at[:, pl.ds(0, HC)], qkv_r.at[:, pl.ds(0, HC)], ps_sem.at[3], pr_sem.at[3], partner)

    send_x.start()

    def project(x, which, dst):
        @pl.loop(0, 2)
        def _(i):
            cols = pl.ds(pl.multiple_of(i * 256, 256), 256)
            dcols = pl.ds(pl.multiple_of(which * HC + i * 256, 256), 256)
            part = jnp.dot(x[...], w[which, :, cols], preferred_element_type=F32)
            dst[:, dcols] = silu(part).astype(BF16)

    def state(qkv, dst):
        for h in range(NH):
            key = qkv[:, pl.ds(HC + h * HD, HD)]
            val = qkv[:, pl.ds(2 * HC + h * HD, HD)]
            kv = lax.dot_general(key, val, (((0,), (0,)), ((), ())), preferred_element_type=F32)
            dst[pl.ds(h * HD, HD), :] = kv.astype(BF16)

    def rows(i):
        return pl.ds(pl.multiple_of(i * SL, SL), SL)

    def scatter_start(kv, got, core, n, first):
        for k in range(first, PLANE):
            j = chip(k)
            remote(kv.at[rows(j)], got.at[p], s1_sem.at[n], q1_sem.at[n], (core, base + j)).start()

    def scatter_wait(kv, got, n, first):
        m = PLANE - first
        remote(kv.at[pl.ds(0, m * SL)], kv.at[pl.ds(0, m * SL)], s1_sem.at[n], q1_sem.at[n], partner).wait_recv()

    def totals_start(got, tot, r2, n):
        total = got[0].astype(F32)
        for i in range(1, PLANE):
            total = total + got[i].astype(F32)
        tot[...] = total.astype(BF16)
        for k in range(1, NZ):
            @pl.when(z + k < NZ)
            def _():
                remote(
                    tot, r2.at[z], s2_sem.at[n, k], q2_sem.at[n, z], (f, (z + k) * PLANE + p)
                ).start()

    def prefix_start(got, tot, r2, o3, pf, n):
        def add(i, total):
            remote(tot, r2.at[i], s2_sem.at[n, 0], q2_sem.at[n, i], partner).wait_recv()
            return total + r2[i].astype(F32)

        total = lax.fori_loop(0, z, add, jnp.zeros((SL, HD), F32))
        for i in range(PLANE):
            o3[i] = total.astype(BF16)
            if i < PLANE - 1:
                total = total + got[i].astype(F32)
        for k in range(1, PLANE):
            j = chip(k)
            remote(o3.at[j], pf.at[rows(p)], s3_sem.at[n], q3_sem.at[n], (f, base + j)).start()
        pf[rows(p), :] = o3[p]

    def prefix_wait(pf, n):
        m = PLANE - 1
        remote(pf.at[pl.ds(0, m * SL)], pf.at[pl.ds(0, m * SL)], s3_sem.at[n], q3_sem.at[n], partner).wait_recv()

    half = T // 2
    tri = lax.broadcasted_iota(jnp.int32, (half, half), 0) >= lax.broadcasted_iota(jnp.int32, (half, half), 1)

    def intra(qkv, y):
        nt = (((1,), (1,)), ((), ()))
        for h in range(NH):
            qc, kc, vc = (pl.ds(n * HC + h * HD, HD) for n in range(3))
            lo, hi = pl.ds(0, half), pl.ds(half, half)
            q0, q1 = qkv[lo, qc], qkv[hi, qc]
            k0, k1 = qkv[lo, kc], qkv[hi, kc]
            v0, v1 = qkv[lo, vc], qkv[hi, vc]
            s00 = lax.dot_general(q0, k0, nt, preferred_element_type=F32)
            s10 = lax.dot_general(q1, k0, nt, preferred_element_type=F32)
            s11 = lax.dot_general(q1, k1, nt, preferred_element_type=F32)
            s00 = jnp.where(tri, s00, 0.0).astype(BF16)
            s11 = jnp.where(tri, s11, 0.0).astype(BF16)
            s10 = s10.astype(BF16)
            yc = pl.ds(h * HD, HD)
            y[lo, yc] = jnp.dot(s00, v0, preferred_element_type=F32)
            y[hi, yc] = jnp.dot(s10, v0, preferred_element_type=F32) + jnp.dot(s11, v1, preferred_element_type=F32)

    def finish(qkv, y, pf, core, dst):
        for h in range(NH):
            cols = pl.ds(h * HD, HD)
            inter = jnp.dot(qkv[:, cols], pf[pl.ds(h * HD, HD), :], preferred_element_type=F32)
            total = y[:, cols] + inter
            scale = lax.rsqrt(jnp.mean(total * total, axis=-1, keepdims=True) + 1e-06)
            dst[:, cols] = (total * scale * gain_ref[pl.ds(core * NH + h, 1), :]).astype(BF16)

    loads[0].wait()
    loads[1].wait()
    project(x_own, 1, qkv_a)
    loads[2].wait()
    project(x_own, 2, qkv_a)
    state(qkv_a, kv_a)
    scatter_start(kv_a, r1a, f, 0, 1)
    r1a[p] = kv_a[rows(p), :]
    send_x.wait_recv()
    send_wo.start()

    project(x_oth, 1, qkv_s)
    project(x_oth, 2, qkv_s)
    state(qkv_s, kv_b)
    scatter_start(kv_b, r1b, g, 1, 0)
    send_k.start()
    scatter_wait(kv_a, r1a, 0, 1)
    totals_start(r1a, t2a, r2a, 0)
    loads[3].wait()
    project(x_oth, 0, qkv_s)
    send_q.start()
    scatter_wait(kv_b, r1b, 1, 0)
    totals_start(r1b, t2b, r2b, 1)
    prefix_start(r1a, t2a, r2a, o3a, pfa, 0)
    project(x_own, 0, qkv_a)
    prefix_start(r1b, t2b, r2b, o3b, pfb, 1)
    intra(qkv_a, y_a)
    send_k.wait_recv()
    send_q.wait_recv()
    intra(qkv_r, y_b)
    prefix_wait(pfa, 0)
    finish(qkv_a, y_a, pfa, f, n_a)
    loads[4].wait()

    @pl.loop(0, 4)
    def _(i):
        cols = pl.ds(pl.multiple_of(i * 512, 512), 512)
        acc[:, cols] = jnp.dot(n_a[...], wo_own[:, cols], preferred_element_type=F32)

    prefix_wait(pfb, 1)
    finish(qkv_r, y_b, pfb, g, n_b)
    send_wo.wait_recv()

    def out_copy(i):
        cols = pl.ds(pl.multiple_of(i * 512, 512), 512)
        return pltpu.make_async_copy(out_v.at[:, cols], out_hbm.at[0, :, cols], st_sem.at[i])

    @pl.loop(0, 4)
    def _(i):
        cols = pl.ds(pl.multiple_of(i * 512, 512), 512)
        mixed = acc[:, cols] + jnp.dot(n_b[...], wo_oth[:, cols], preferred_element_type=F32)
        out_v[:, cols] = mixed.astype(BF16)
        out_copy(i).start()

    for copy in (send_x, send_wo, send_k, send_q):
        copy.wait_send()
    for n, first in ((0, 1), (1, 0)):
        kv = (kv_a, kv_b)[n]
        span = pl.ds(0, (PLANE - first) * SL)
        remote(kv.at[span], kv.at[span], s1_sem.at[n], q1_sem.at[n], partner).wait_send()
        span = pl.ds(0, (PLANE - 1) * SL)
        remote(kv.at[span], kv.at[span], s3_sem.at[n], q3_sem.at[n], partner).wait_send()
        tot = (t2a, t2b)[n]
        for k in range(1, NZ):
            @pl.when(z + k < NZ)
            def _():
                remote(tot, tot, s2_sem.at[n, k], q2_sem.at[n, k], partner).wait_send()
    for i in range(4):
        out_copy(i).wait()


def body(tokens, w_qkv, w_out, gain):
    w = jnp.transpose(w_qkv, (1, 0, 2))
    any_ = pl.BlockSpec(memory_space=pl.ANY)
    vm = pltpu.VMEM
    dma = pltpu.SemaphoreType.DMA
    scratch = [
        vm((T, D), BF16), vm((T, D), BF16), vm((3, D, HC), BF16), vm((HC, D), BF16), vm((HC, D), BF16),
        vm((T, 3 * HC), BF16), vm((T, 3 * HC), BF16), vm((T, 3 * HC), BF16),
        vm((HC, HD), BF16), vm((HC, HD), BF16),
        vm((PLANE, SL, HD), BF16), vm((PLANE, SL, HD), BF16),
        vm((SL, HD), BF16), vm((SL, HD), BF16),
        vm((NZ, SL, HD), BF16), vm((NZ, SL, HD), BF16),
        vm((PLANE, SL, HD), BF16), vm((PLANE, SL, HD), BF16),
        vm((HC, HD), BF16), vm((HC, HD), BF16),
        vm((T, HC), F32), vm((T, HC), F32), vm((T, HC), BF16), vm((T, HC), BF16),
        vm((T, D), F32), vm((T, D), BF16),
        dma((5,)), dma((4,)), dma((4,)), dma((4,)),
        dma((2,)), dma((2,)), dma((2, NZ)), dma((2, NZ)), dma((2,)), dma((2,)),
    ]
    return pl.pallas_call(
        kernel,
        out_shape=jax.ShapeDtypeStruct((1, T, D), BF16),
        in_specs=[any_, any_, any_, pl.BlockSpec(memory_space=pltpu.VMEM)],
        out_specs=any_,
        scratch_shapes=scratch,
        compiler_params=pltpu.CompilerParams(
            collective_id=0, has_side_effects=True, vmem_limit_bytes=56 * 1024 * 1024
        ),
        cost_estimate=pl.CostEstimate(flops=10_000_000_000, bytes_accessed=14_000_000, transcendentals=1_600_000),
    )(tokens, w, w_out, gain.reshape(2 * NH, HD))


def solution(mesh):
    in_specs = (P("fsdp", "ctx", None), P(None, None, "fsdp"), P("fsdp", None), P())
    out_specs = P("fsdp", "ctx", None)
    return jax.shard_map(body, mesh=mesh, in_specs=in_specs, out_specs=out_specs, check_vma=False)
```

time: 585 us -> 36.7 us (0.06)
  the two profiles are of different devices: /device:TPU:224 before, /device:TPU:1 now
where the time goes in v1:
time: 36.7 us; the launch traced here: 36.6 us
  Pallas kernels  33.4 us (91%)
  local copies, waits for them, and re-layouts  3.16 us (9%)
    pallas_call x1, Pallas kernels, body(): pl.pallas_call(kernel, out_shape=jax.ShapeDtypeStruct((1, T, D), BF16), i...  33.4 us
    unnamed x1, local copies, waits for them, and re-layouts  3.16 us

profile of v1, /device:TPU:1, one launch (start us, length us, event | category | flops | bytes accessed | tf_op | source)
XLA Modules:
  0.0 36.6 jit_solution(15232390959714336440)
XLA Ops:
  0.0 33.4 %shard_map.46 = bf16[1,512,2048]{2,1,0:T(8,128)(2,1)} custom-call(bf16[1,512,2048]{2,1,0:T(8,128)(2,1)} %x_hbm.1, bf16[3,2048,512]{2,1,0:T(8,128)(2,1)} %bitcast.2, bf16[512,2048]{1,0:T(8,128)(2,1)} %wo_hbm.1, f32[8,128]{1,0:T(8,128)} %bitcast.3), custom_call_target="tpu_custom_call" | custom-call | flops 10000000000 | bytes 14000000 | tf_op jit(solution)/shard_map/pallas_call | solution.py:256
  33.4 3.2 %copy.6 = bf16[1,512,2048]{2,1,0:T(8,128)(2,1)} copy(bf16[1,512,2048]{2,1,0:T(8,128)(2,1)} %shard_map.46) | data formatting | bytes 4194304

commit v2 on v1

--- a/solution.py
+++ b/solution.py
@@ -16,6 +16,8 @@
 F32 = jnp.float32
 BF16 = jnp.bfloat16
 MESH = pl.DeviceIdType.MESH
+FAR = sorted(((dx, dy) for dx in range(4) for dy in range(4)), key=lambda o: -min(o[0], 4 - o[0]) - min(o[1], 4 - o[1]))
+FARZ = (4, 3, 5, 2, 6, 1, 7)
 
 
 def silu(v):
@@ -30,12 +32,13 @@
 
 
 def kernel(
-    x_hbm, w_hbm, wo_hbm, gain_ref, out_hbm,
-    x_own, x_oth, w, wo_own, wo_oth,
+    x_hbm, w_hbm, wo_hbm, gain_hbm,
+    acc, n_b, wo_oth,
+    x_own, x_oth, w, wo_own, gain_ref,
     qkv_a, qkv_s, qkv_r,
     kv_a, kv_b, r1a, r1b, t2a, t2b, r2a, r2b, o3a, o3b, pfa, pfb,
-    y_a, y_b, n_a, n_b, acc, out_v,
-    ld_sem, st_sem, ps_sem, pr_sem, s1_sem, q1_sem, s2_sem, q2_sem, s3_sem, q3_sem,
+    y_a, y_b, n_a,
+    ld_sem, ps_sem, pr_sem, s1_sem, q1_sem, s2_sem, q2_sem, s3_sem, q3_sem,
 ):
     f = lax.axis_index("fsdp")
     c = lax.axis_index("ctx")
@@ -44,45 +47,46 @@
     base = z * PLANE
     g = 1 - f
 
+    px, py = p // 4, lax.rem(p, 4)
+
     def chip(k):
-        return lax.rem(p + k, PLANE)
+        dx, dy = FAR[k]
+        return lax.rem(px + dx, 4) * 4 + lax.rem(py + dy, 4)
+
+    def plane(k):
+        return lax.rem(z + FARZ[k], NZ) * PLANE + p
 
     barrier = pltpu.get_barrier_semaphore()
     for k in range(PLANE):
+        if k < NZ - 1:
+            pl.semaphore_signal(barrier, inc=1, device_id=(f, plane(k)), device_id_type=MESH)
         pl.semaphore_signal(barrier, inc=1, device_id=(g, base + chip(k)), device_id_type=MESH)
-        if k:
+        if k < PLANE - 1:
             pl.semaphore_signal(barrier, inc=1, device_id=(f, base + chip(k)), device_id_type=MESH)
-    for k in range(1, NZ):
-        pl.semaphore_signal(
-            barrier, inc=1, device_id=(f, lax.rem(z + k, NZ) * PLANE + p), device_id_type=MESH
-        )
 
     loads = [pltpu.make_async_copy(x_hbm.at[0], x_own, ld_sem.at[0])]
     for n, which in enumerate((1, 2, 0)):
         loads.append(pltpu.make_async_copy(w_hbm.at[which], w.at[which], ld_sem.at[1 + n]))
     loads.append(pltpu.make_async_copy(wo_hbm, wo_own, ld_sem.at[4]))
+    loads.append(pltpu.make_async_copy(gain_hbm, gain_ref, ld_sem.at[5]))
     for copy in loads:
         copy.start()
 
-    pl.semaphore_wait(barrier, 2 * PLANE - 1 + NZ - 1)
-
     partner = (g, c)
-    send_x = remote(x_hbm.at[0], x_oth, ps_sem.at[0], pr_sem.at[0], partner)
+    halves = [pl.ds(0, T // 2), pl.ds(T // 2, T // 2)]
+    send_x = [
+        remote(x_hbm.at[0, half], x_oth.at[half], ps_sem.at[4 + n], pr_sem.at[4 + n], partner)
+        for n, half in enumerate(halves)
+    ]
     send_wo = remote(wo_hbm, wo_oth, ps_sem.at[1], pr_sem.at[1], partner)
     send_k = remote(
         qkv_s.at[:, pl.ds(HC, 2 * HC)], qkv_r.at[:, pl.ds(HC, 2 * HC)], ps_sem.at[2], pr_sem.at[2], partner
     )
     send_q = remote(qkv_s.at[:, pl.ds(0, HC)], qkv_r.at[:, pl.ds(0, HC)], ps_sem.at[3], pr_sem.at[3], partner)
 
-    send_x.start()
-
-    def project(x, which, dst):
-        @pl.loop(0, 2)
-        def _(i):
-            cols = pl.ds(pl.multiple_of(i * 256, 256), 256)
-            dcols = pl.ds(pl.multiple_of(which * HC + i * 256, 256), 256)
-            part = jnp.dot(x[...], w[which, :, cols], preferred_element_type=F32)
-            dst[:, dcols] = silu(part).astype(BF16)
+    def project(x, which, dst, rows=pl.ds(0, T)):
+        part = jnp.dot(x[rows, :], w[which], preferred_element_type=F32)
+        dst[rows, pl.ds(which * HC, HC)] = silu(part).astype(BF16)
 
     def state(qkv, dst):
         for h in range(NH):
@@ -95,7 +99,7 @@
         return pl.ds(pl.multiple_of(i * SL, SL), SL)
 
     def scatter_start(kv, got, core, n, first):
-        for k in range(first, PLANE):
+        for k in range(PLANE - first):
             j = chip(k)
             remote(kv.at[rows(j)], got.at[p], s1_sem.at[n], q1_sem.at[n], (core, base + j)).start()
 
@@ -108,7 +112,7 @@
         for i in range(1, PLANE):
             total = total + got[i].astype(F32)
         tot[...] = total.astype(BF16)
-        for k in range(1, NZ):
+        for k in (4, 3, 5, 2, 6, 1, 7):
             @pl.when(z + k < NZ)
             def _():
                 remote(
@@ -125,7 +129,7 @@
             o3[i] = total.astype(BF16)
             if i < PLANE - 1:
                 total = total + got[i].astype(F32)
-        for k in range(1, PLANE):
+        for k in range(PLANE - 1):
             j = chip(k)
             remote(o3.at[j], pf.at[rows(p)], s3_sem.at[n], q3_sem.at[n], (f, base + j)).start()
         pf[rows(p), :] = o3[p]
@@ -166,34 +170,39 @@
     loads[0].wait()
     loads[1].wait()
     project(x_own, 1, qkv_a)
+    pl.semaphore_wait(barrier, 2 * PLANE - 1 + NZ - 1)
+    for copy in send_x:
+        copy.start()
     loads[2].wait()
     project(x_own, 2, qkv_a)
     state(qkv_a, kv_a)
     scatter_start(kv_a, r1a, f, 0, 1)
     r1a[p] = kv_a[rows(p), :]
-    send_x.wait_recv()
-    send_wo.start()
-
-    project(x_oth, 1, qkv_s)
-    project(x_oth, 2, qkv_s)
+    loads[3].wait()
+    project(x_own, 0, qkv_a)
+
+    for copy, half_rows in zip(send_x, halves):
+        copy.wait_recv()
+        project(x_oth, 1, qkv_s, half_rows)
+        project(x_oth, 2, qkv_s, half_rows)
     state(qkv_s, kv_b)
     scatter_start(kv_b, r1b, g, 1, 0)
     send_k.start()
+    project(x_oth, 0, qkv_s)
+    send_q.start()
+    send_wo.start()
     scatter_wait(kv_a, r1a, 0, 1)
     totals_start(r1a, t2a, r2a, 0)
-    loads[3].wait()
-    project(x_oth, 0, qkv_s)
-    send_q.start()
+    intra(qkv_a, y_a)
     scatter_wait(kv_b, r1b, 1, 0)
     totals_start(r1b, t2b, r2b, 1)
     prefix_start(r1a, t2a, r2a, o3a, pfa, 0)
-    project(x_own, 0, qkv_a)
-    prefix_start(r1b, t2b, r2b, o3b, pfb, 1)
-    intra(qkv_a, y_a)
     send_k.wait_recv()
     send_q.wait_recv()
     intra(qkv_r, y_b)
+    prefix_start(r1b, t2b, r2b, o3b, pfb, 1)
     prefix_wait(pfa, 0)
+    loads[5].wait()
     finish(qkv_a, y_a, pfa, f, n_a)
     loads[4].wait()
 
@@ -202,36 +211,30 @@
         cols = pl.ds(pl.multiple_of(i * 512, 512), 512)
         acc[:, cols] = jnp.dot(n_a[...], wo_own[:, cols], preferred_element_type=F32)
 
-    prefix_wait(pfb, 1)
-    finish(qkv_r, y_b, pfb, g, n_b)
     send_wo.wait_recv()
-
-    def out_copy(i):
-        cols = pl.ds(pl.multiple_of(i * 512, 512), 512)
-        return pltpu.make_async_copy(out_v.at[:, cols], out_hbm.at[0, :, cols], st_sem.at[i])
-
-    @pl.loop(0, 4)
-    def _(i):
-        cols = pl.ds(pl.multiple_of(i * 512, 512), 512)
-        mixed = acc[:, cols] + jnp.dot(n_b[...], wo_oth[:, cols], preferred_element_type=F32)
-        out_v[:, cols] = mixed.astype(BF16)
-        out_copy(i).start()
-
-    for copy in (send_x, send_wo, send_k, send_q):
+    for copy in (*send_x, send_wo, send_k, send_q):
         copy.wait_send()
     for n, first in ((0, 1), (1, 0)):
         kv = (kv_a, kv_b)[n]
         span = pl.ds(0, (PLANE - first) * SL)
         remote(kv.at[span], kv.at[span], s1_sem.at[n], q1_sem.at[n], partner).wait_send()
-        span = pl.ds(0, (PLANE - 1) * SL)
-        remote(kv.at[span], kv.at[span], s3_sem.at[n], q3_sem.at[n], partner).wait_send()
         tot = (t2a, t2b)[n]
         for k in range(1, NZ):
             @pl.when(z + k < NZ)
             def _():
                 remote(tot, tot, s2_sem.at[n, k], q2_sem.at[n, k], partner).wait_send()
-    for i in range(4):
-        out_copy(i).wait()
+
+    prefix_wait(pfb, 1)
+    finish(qkv_r, y_b, pfb, g, n_b)
+    span = pl.ds(0, (PLANE - 1) * SL)
+    for n in range(2):
+        remote(kv_a.at[span], kv_a.at[span], s3_sem.at[n], q3_sem.at[n], partner).wait_send()
+
+
+def out_kernel(acc, n_b, wo_oth, out):
+    cols = pl.ds(pl.multiple_of(pl.program_id(0) * 512, 512), 512)
+    mixed = acc[:, cols] + jnp.dot(n_b[...], wo_oth[:, cols], preferred_element_type=F32)
+    out[0] = mixed.astype(BF16)
 
 
 def body(tokens, w_qkv, w_out, gain):
@@ -240,7 +243,7 @@
     vm = pltpu.VMEM
     dma = pltpu.SemaphoreType.DMA
     scratch = [
-        vm((T, D), BF16), vm((T, D), BF16), vm((3, D, HC), BF16), vm((HC, D), BF16), vm((HC, D), BF16),
+        vm((T, D), BF16), vm((T, D), BF16), vm((3, D, HC), BF16), vm((HC, D), BF16), vm((2 * NH, HD), F32),
         vm((T, 3 * HC), BF16), vm((T, 3 * HC), BF16), vm((T, 3 * HC), BF16),
         vm((HC, HD), BF16), vm((HC, HD), BF16),
         vm((PLANE, SL, HD), BF16), vm((PLANE, SL, HD), BF16),
@@ -248,22 +251,31 @@
         vm((NZ, SL, HD), BF16), vm((NZ, SL, HD), BF16),
         vm((PLANE, SL, HD), BF16), vm((PLANE, SL, HD), BF16),
         vm((HC, HD), BF16), vm((HC, HD), BF16),
-        vm((T, HC), F32), vm((T, HC), F32), vm((T, HC), BF16), vm((T, HC), BF16),
-        vm((T, D), F32), vm((T, D), BF16),
-        dma((5,)), dma((4,)), dma((4,)), dma((4,)),
+        vm((T, HC), F32), vm((T, HC), F32), vm((T, HC), BF16),
+        dma((6,)), dma((6,)), dma((6,)),
         dma((2,)), dma((2,)), dma((2, NZ)), dma((2, NZ)), dma((2,)), dma((2,)),
     ]
-    return pl.pallas_call(
+    whole = pl.BlockSpec(memory_space=pltpu.VMEM)
+    acc, n_b, wo_oth = pl.pallas_call(
         kernel,
-        out_shape=jax.ShapeDtypeStruct((1, T, D), BF16),
-        in_specs=[any_, any_, any_, pl.BlockSpec(memory_space=pltpu.VMEM)],
-        out_specs=any_,
+        out_shape=[pltpu.VMEM((T, D), F32), pltpu.VMEM((T, HC), BF16), pltpu.VMEM((HC, D), BF16)],
+        in_specs=[any_] * 4,
+        out_specs=[whole, whole, whole],
         scratch_shapes=scratch,
         compiler_params=pltpu.CompilerParams(
-            collective_id=0, has_side_effects=True, vmem_limit_bytes=56 * 1024 * 1024
+            collective_id=0, has_side_effects=True, vmem_limit_bytes=32 * 1024 * 1024
         ),
-        cost_estimate=pl.CostEstimate(flops=10_000_000_000, bytes_accessed=14_000_000, transcendentals=1_600_000),
-    )(tokens, w, w_out, gain.reshape(2 * NH, HD))
+        cost_estimate=pl.CostEstimate(flops=9_000_000_000, bytes_accessed=12_000_000, transcendentals=1_600_000),
+    )(*(pltpu.with_memory_space_constraint(a, pltpu.HBM) for a in (tokens, w, w_out, gain.reshape(2 * NH, HD))))
+    return pl.pallas_call(
+        out_kernel,
+        out_shape=jax.ShapeDtypeStruct((1, T, D), BF16),
+        grid=(4,),
+        in_specs=[whole, whole, whole],
+        out_specs=pl.BlockSpec((1, T, 512), lambda i: (0, 0, i)),
+        compiler_params=pltpu.CompilerParams(vmem_limit_bytes=16 * 1024 * 1024),
+        cost_estimate=pl.CostEstimate(flops=1_000_000_000, bytes_accessed=2_000_000, transcendentals=0),
+    )(acc, n_b, wo_oth)
 
 
 def solution(mesh):

time: 36.7 us -> 31.2 us (0.85)
  local copies, waits for them, and re-layouts: 3.16 us -> 0 us
  Pallas kernels: 33.4 us -> 31.1 us
    unnamed x1 -> x0, local copies, waits for them, and re-layouts: 3.16 us -> none
    pallas_call x1 -> x2, Pallas kernels: 33.4 us -> 31.1 us  [the longest x1 28.2 us: body(): pl.pallas_call(kernel, out_shape=[pltpu.VMEM((T, D), F32), pltpu.VMEM((T,...]
where the time goes in v2:
time: 31.2 us; the launch traced here: 31.1 us
  Pallas kernels  31.1 us (100%)
    pallas_call x1, Pallas kernels, body(): pl.pallas_call(kernel, out_shape=[pltpu.VMEM((T, D), F32), pltpu.VMEM((T,...  28.2 us
    pallas_call x1, Pallas kernels, body(): pl.pallas_call(out_kernel, out_shape=jax.ShapeDtypeStruct((1, T, D), BF16...  2.94 us

profile of v2, /device:TPU:1, one launch (start us, length us, event | category | flops | bytes accessed | tf_op | source)
XLA Modules:
  0.0 31.1 jit_solution(18247292058915469890)
XLA Ops:
  0.0 28.2 %shard_map.46 = (f32[512,2048]{1,0:T(8,128)S(1)}, bf16[512,512]{1,0:T(8,128)(2,1)S(1)}, bf16[512,2048]{1,0:T(8,128)(2,1)S(1)}) custom-call(bf16[1,512,2048]{2,1,0:T(8,128)(2,1)} %x_hbm.1, bf16[3,2048,512]{2,1,0:T(8,128)(2,1)} %bitcast.2, bf16[512,2048]{1,0:T(8,128)(2,1)} %wo_hbm.1, f32[8,128]{1,0:T(8,128)} %bitcast.3), custom_call_target="tpu_custom_call" | custom-call | flops 8999999488 | bytes 12000000 | tf_op jit(solution)/shard_map/pallas_call | solution.py:259
  28.2 2.9 %shard_map.47 = bf16[1,512,2048]{2,1,0:T(8,128)(2,1)} custom-call(f32[512,2048]{1,0:T(8,128)S(1)} %get-tuple-element.8.acc, bf16[512,512]{1,0:T(8,128)(2,1)S(1)} %get-tuple-element.9.n_b, bf16[512,2048]{1,0:T(8,128)(2,1)S(1)} %get-tuple-element.10.wo_oth), custom_call_target="tpu_custom_call" | custom-call | flops 1000000000 | bytes 2000000 | tf_op jit(solution)/shard_map/pallas_call | solution.py:270

commit v3 on v2

--- a/solution.py
+++ b/solution.py
@@ -17,7 +17,6 @@
 BF16 = jnp.bfloat16
 MESH = pl.DeviceIdType.MESH
 FAR = sorted(((dx, dy) for dx in range(4) for dy in range(4)), key=lambda o: -min(o[0], 4 - o[0]) - min(o[1], 4 - o[1]))
-FARZ = (4, 3, 5, 2, 6, 1, 7)
 
 
 def silu(v):
@@ -38,7 +37,7 @@
     qkv_a, qkv_s, qkv_r,
     kv_a, kv_b, r1a, r1b, t2a, t2b, r2a, r2b, o3a, o3b, pfa, pfb,
     y_a, y_b, n_a,
-    ld_sem, ps_sem, pr_sem, s1_sem, q1_sem, s2_sem, q2_sem, s3_sem, q3_sem,
+    ld_sem, ps_sem, pr_sem, s1_sem, q1_sem, s2_sem, q2_sem, s3_sem, q3_sem, in_sem,
 ):
     f = lax.axis_index("fsdp")
     c = lax.axis_index("ctx")
@@ -53,16 +52,21 @@
         dx, dy = FAR[k]
         return lax.rem(px + dx, 4) * 4 + lax.rem(py + dy, 4)
 
-    def plane(k):
-        return lax.rem(z + FARZ[k], NZ) * PLANE + p
-
+    def tell(sem, core, plane, spot):
+        pl.semaphore_signal(sem, inc=1, device_id=(core, plane * PLANE + spot), device_id_type=MESH)
+
+    def at(dx, dy):
+        return lax.rem(px + dx, 4) * 4 + lax.rem(py + dy, 4)
+
+    near = ((1, 0), (3, 0), (0, 1), (0, 3))
     barrier = pltpu.get_barrier_semaphore()
-    for k in range(PLANE):
-        if k < NZ - 1:
-            pl.semaphore_signal(barrier, inc=1, device_id=(f, plane(k)), device_id_type=MESH)
-        pl.semaphore_signal(barrier, inc=1, device_id=(g, base + chip(k)), device_id_type=MESH)
-        if k < PLANE - 1:
-            pl.semaphore_signal(barrier, inc=1, device_id=(f, base + chip(k)), device_id_type=MESH)
+    tell(barrier, g, z, p)
+    for dx, dy in near:
+        tell(barrier, f, z, at(dx, dy))
+    for k in (4, 3, 5, 2, 6, 1, 7):
+        @pl.when(z + k < NZ)
+        def _():
+            tell(barrier, f, z + k, p)
 
     loads = [pltpu.make_async_copy(x_hbm.at[0], x_own, ld_sem.at[0])]
     for n, which in enumerate((1, 2, 0)):
@@ -167,40 +171,60 @@
             scale = lax.rsqrt(jnp.mean(total * total, axis=-1, keepdims=True) + 1e-06)
             dst[:, cols] = (total * scale * gain_ref[pl.ds(core * NH + h, 1), :]).astype(BF16)
 
+    pl.semaphore_wait(barrier, 5 + z)
+    for copy in send_x:
+        copy.start()
+    tell(in_sem.at[0], g, z, p)
+    for dx, dy in near:
+        tell(in_sem.at[0], f, z, at(dx, dy))
+    for k in (4, 3, 5, 2, 6, 1, 7):
+        @pl.when(z - k >= 0)
+        def _():
+            tell(in_sem.at[3], f, z - k, p)
+
     loads[0].wait()
     loads[1].wait()
     project(x_own, 1, qkv_a)
-    pl.semaphore_wait(barrier, 2 * PLANE - 1 + NZ - 1)
-    for copy in send_x:
-        copy.start()
+    pl.semaphore_wait(in_sem.at[0], 5)
+    tell(in_sem.at[1], f, z, at(2, 0))
+    tell(in_sem.at[1], f, z, at(0, 2))
+    tell(in_sem.at[1], g, z, p)
     loads[2].wait()
     project(x_own, 2, qkv_a)
     state(qkv_a, kv_a)
+    pl.semaphore_wait(in_sem.at[1], 3)
+    tell(in_sem.at[2], g, z, p)
     scatter_start(kv_a, r1a, f, 0, 1)
     r1a[p] = kv_a[rows(p), :]
-    loads[3].wait()
-    project(x_own, 0, qkv_a)
 
     for copy, half_rows in zip(send_x, halves):
         copy.wait_recv()
         project(x_oth, 1, qkv_s, half_rows)
         project(x_oth, 2, qkv_s, half_rows)
     state(qkv_s, kv_b)
+    pl.semaphore_wait(in_sem.at[2], 1)
     scatter_start(kv_b, r1b, g, 1, 0)
     send_k.start()
+    loads[3].wait()
     project(x_oth, 0, qkv_s)
     send_q.start()
     send_wo.start()
+    project(x_own, 0, qkv_a)
     scatter_wait(kv_a, r1a, 0, 1)
+
+    @pl.when(z < NZ - 1)
+    def _():
+        pl.semaphore_wait(in_sem.at[3], NZ - 1 - z)
+
     totals_start(r1a, t2a, r2a, 0)
     intra(qkv_a, y_a)
     scatter_wait(kv_b, r1b, 1, 0)
     totals_start(r1b, t2b, r2b, 1)
     prefix_start(r1a, t2a, r2a, o3a, pfa, 0)
+    prefix_start(r1b, t2b, r2b, o3b, pfb, 1)
     send_k.wait_recv()
     send_q.wait_recv()
     intra(qkv_r, y_b)
-    prefix_start(r1b, t2b, r2b, o3b, pfb, 1)
     prefix_wait(pfa, 0)
     loads[5].wait()
     finish(qkv_a, y_a, pfa, f, n_a)
@@ -254,6 +278,7 @@
         vm((T, HC), F32), vm((T, HC), F32), vm((T, HC), BF16),
         dma((6,)), dma((6,)), dma((6,)),
         dma((2,)), dma((2,)), dma((2, NZ)), dma((2, NZ)), dma((2,)), dma((2,)),
+        pltpu.SemaphoreType.REGULAR((4,)),
     ]
     whole = pl.BlockSpec(memory_space=pltpu.VMEM)
     acc, n_b, wo_oth = pl.pallas_call(

time: 31.2 us -> 28.3 us (0.907)
  the two profiles are of different devices: /device:TPU:1 before, /device:TPU:224 now
where the time goes in v3:
time: 28.3 us; the launch traced here: 28.2 us
  Pallas kernels  28.2 us (100%)
    pallas_call x1, Pallas kernels, body(): pl.pallas_call(kernel, out_shape=[pltpu.VMEM((T, D), F32), pltpu.VMEM((T,...  25.3 us
    pallas_call x1, Pallas kernels, body(): pl.pallas_call(out_kernel, out_shape=jax.ShapeDtypeStruct((1, T, D), BF16...  2.94 us

profile of v3, /device:TPU:224, one launch (start us, length us, event | category | flops | bytes accessed | tf_op | source)
XLA Modules:
  0.0 28.2 jit_solution(1313586785438925926)
XLA Ops:
  0.0 25.3 %shard_map.46 = (f32[512,2048]{1,0:T(8,128)S(1)}, bf16[512,512]{1,0:T(8,128)(2,1)S(1)}, bf16[512,2048]{1,0:T(8,128)(2,1)S(1)}) custom-call(bf16[1,512,2048]{2,1,0:T(8,128)(2,1)} %x_hbm.1, bf16[3,2048,512]{2,1,0:T(8,128)(2,1)} %bitcast.2, bf16[512,2048]{1,0:T(8,128)(2,1)} %wo_hbm.1, f32[8,128]{1,0:T(8,128)} %bitcast.3), custom_call_target="tpu_custom_call" | custom-call | flops 8999999488 | bytes 12000000 | tf_op jit(solution)/shard_map/pallas_call | solution.py:284
  25.3 2.9 %shard_map.47 = bf16[1,512,2048]{2,1,0:T(8,128)(2,1)} custom-call(f32[512,2048]{1,0:T(8,128)S(1)} %get-tuple-element.8.acc, bf16[512,512]{1,0:T(8,128)(2,1)S(1)} %get-tuple-element.9.n_b, bf16[512,2048]{1,0:T(8,128)(2,1)S(1)} %get-tuple-element.10.wo_oth), custom_call_target="tpu_custom_call" | custom-call | flops 1000000000 | bytes 2000000 | tf_op jit(solution)/shard_map/pallas_call | solution.py:295

commit v4 on v3

--- a/solution.py
+++ b/solution.py
@@ -16,6 +16,7 @@
 F32 = jnp.float32
 BF16 = jnp.bfloat16
 MESH = pl.DeviceIdType.MESH
+WIDTHS = (512, 512, 512, 256, 256)
 FAR = sorted(((dx, dy) for dx in range(4) for dy in range(4)), key=lambda o: -min(o[0], 4 - o[0]) - min(o[1], 4 - o[1]))
 
 
@@ -30,13 +31,22 @@
     )
 
 
+def finish(qkv, y, pf, gain, row, dst):
+    for h in range(NH):
+        cols = pl.ds(h * HD, HD)
+        inter = jnp.dot(qkv[:, cols], pf[cols, :], preferred_element_type=F32)
+        total = y[:, cols] + inter
+        scale = lax.rsqrt(jnp.mean(total * total, axis=-1, keepdims=True) + 1e-06)
+        dst[:, cols] = (total * scale * gain[pl.ds(row + h, 1), :]).astype(BF16)
+
+
 def kernel(
     x_hbm, w_hbm, wo_hbm, gain_hbm,
-    acc, n_b, wo_oth,
+    acc, y_b, qkv_r, pfb, gain_b, wo_oth,
     x_own, x_oth, w, wo_own, gain_ref,
-    qkv_a, qkv_s, qkv_r,
-    kv_a, kv_b, r1a, r1b, t2a, t2b, r2a, r2b, o3a, o3b, pfa, pfb,
-    y_a, y_b, n_a,
+    qkv_a, qkv_s,
+    kv_a, kv_b, r1a, r1b, t2a, t2b, r2a, r2b, o3a, o3b, pfa, kv_sum,
+    y_a, n_a,
     ld_sem, ps_sem, pr_sem, s1_sem, q1_sem, s2_sem, q2_sem, s3_sem, q3_sem, in_sem,
 ):
     f = lax.axis_index("fsdp")
@@ -57,6 +67,16 @@
 
     def at(dx, dy):
         return lax.rem(px + dx, 4) * 4 + lax.rem(py + dy, 4)
+
+    halves = [pl.ds(0, T // 2), pl.ds(T // 2, T // 2)]
+    sources = (
+        (x_hbm.at[0, halves[0]], x_own.at[halves[0]]), (w_hbm.at[1], w.at[1]),
+        (x_hbm.at[0, halves[1]], x_own.at[halves[1]]), (w_hbm.at[2], w.at[2]),
+        (w_hbm.at[0], w.at[0]), (wo_hbm, wo_own), (gain_hbm, gain_ref),
+    )
+    loads = [pltpu.make_async_copy(src, dst, ld_sem.at[n]) for n, (src, dst) in enumerate(sources)]
+    for copy in loads[:4]:
+        copy.start()
 
     near = ((1, 0), (3, 0), (0, 1), (0, 3))
     barrier = pltpu.get_barrier_semaphore()
@@ -68,19 +88,11 @@
         def _():
             tell(barrier, f, z + k, p)
 
-    loads = [pltpu.make_async_copy(x_hbm.at[0], x_own, ld_sem.at[0])]
-    for n, which in enumerate((1, 2, 0)):
-        loads.append(pltpu.make_async_copy(w_hbm.at[which], w.at[which], ld_sem.at[1 + n]))
-    loads.append(pltpu.make_async_copy(wo_hbm, wo_own, ld_sem.at[4]))
-    loads.append(pltpu.make_async_copy(gain_hbm, gain_ref, ld_sem.at[5]))
-    for copy in loads:
-        copy.start()
-
     partner = (g, c)
-    halves = [pl.ds(0, T // 2), pl.ds(T // 2, T // 2)]
+    parts = [pl.ds(0, T // 2), pl.ds(T // 2, T // 4), pl.ds(3 * T // 4, T // 4)]
     send_x = [
         remote(x_hbm.at[0, half], x_oth.at[half], ps_sem.at[4 + n], pr_sem.at[4 + n], partner)
-        for n, half in enumerate(halves)
+        for n, half in enumerate(parts)
     ]
     send_wo = remote(wo_hbm, wo_oth, ps_sem.at[1], pr_sem.at[1], partner)
     send_k = remote(
@@ -92,12 +104,18 @@
         part = jnp.dot(x[rows, :], w[which], preferred_element_type=F32)
         dst[rows, pl.ds(which * HC, HC)] = silu(part).astype(BF16)
 
-    def state(qkv, dst):
+    def state(qkv, dst, part=pl.ds(0, T), first=True, last=True):
         for h in range(NH):
-            key = qkv[:, pl.ds(HC + h * HD, HD)]
-            val = qkv[:, pl.ds(2 * HC + h * HD, HD)]
+            key = qkv[part, pl.ds(HC + h * HD, HD)]
+            val = qkv[part, pl.ds(2 * HC + h * HD, HD)]
             kv = lax.dot_general(key, val, (((0,), (0,)), ((), ())), preferred_element_type=F32)
-            dst[pl.ds(h * HD, HD), :] = kv.astype(BF16)
+            head = pl.ds(h * HD, HD)
+            if not first:
+                kv = kv + kv_sum[head, :]
+            if last:
+                dst[head, :] = kv.astype(BF16)
+            else:
+                kv_sum[head, :] = kv
 
     def rows(i):
         return pl.ds(pl.multiple_of(i * SL, SL), SL)
@@ -163,16 +181,8 @@
             y[lo, yc] = jnp.dot(s00, v0, preferred_element_type=F32)
             y[hi, yc] = jnp.dot(s10, v0, preferred_element_type=F32) + jnp.dot(s11, v1, preferred_element_type=F32)
 
-    def finish(qkv, y, pf, core, dst):
-        for h in range(NH):
-            cols = pl.ds(h * HD, HD)
-            inter = jnp.dot(qkv[:, cols], pf[pl.ds(h * HD, HD), :], preferred_element_type=F32)
-            total = y[:, cols] + inter
-            scale = lax.rsqrt(jnp.mean(total * total, axis=-1, keepdims=True) + 1e-06)
-            dst[:, cols] = (total * scale * gain_ref[pl.ds(core * NH + h, 1), :]).astype(BF16)
-
     pl.semaphore_wait(barrier, 5 + z)
-    for copy in send_x:
+    for copy in (*send_x, *loads[4:]):
         copy.start()
     tell(in_sem.at[0], g, z, p)
     for dx, dy in near:
@@ -182,14 +192,17 @@
         def _():
             tell(in_sem.at[3], f, z - k, p)
 
-    loads[0].wait()
-    loads[1].wait()
-    project(x_own, 1, qkv_a)
+    for n in range(2):
+        loads[n].wait()
+        if n:
+            project(x_own, 1, qkv_a, halves[0])
+    loads[2].wait()
+    project(x_own, 1, qkv_a, halves[1])
     pl.semaphore_wait(in_sem.at[0], 5)
     tell(in_sem.at[1], f, z, at(2, 0))
     tell(in_sem.at[1], f, z, at(0, 2))
     tell(in_sem.at[1], g, z, p)
-    loads[2].wait()
+    loads[3].wait()
     project(x_own, 2, qkv_a)
     state(qkv_a, kv_a)
     pl.semaphore_wait(in_sem.at[1], 3)
@@ -197,15 +210,15 @@
     scatter_start(kv_a, r1a, f, 0, 1)
     r1a[p] = kv_a[rows(p), :]
 
-    for copy, half_rows in zip(send_x, halves):
+    for n, (copy, part) in enumerate(zip(send_x, parts)):
         copy.wait_recv()
-        project(x_oth, 1, qkv_s, half_rows)
-        project(x_oth, 2, qkv_s, half_rows)
-    state(qkv_s, kv_b)
+        project(x_oth, 1, qkv_s, part)
+        project(x_oth, 2, qkv_s, part)
+        state(qkv_s, kv_b, part, n == 0, n == 2)
     pl.semaphore_wait(in_sem.at[2], 1)
     scatter_start(kv_b, r1b, g, 1, 0)
     send_k.start()
-    loads[3].wait()
+    loads[4].wait()
     project(x_oth, 0, qkv_s)
     send_q.start()
     send_wo.start()
@@ -226,14 +239,14 @@
     send_q.wait_recv()
     intra(qkv_r, y_b)
     prefix_wait(pfa, 0)
+    loads[6].wait()
+    finish(qkv_a, y_a, pfa, gain_ref, f * NH, n_a)
     loads[5].wait()
-    finish(qkv_a, y_a, pfa, f, n_a)
-    loads[4].wait()
-
-    @pl.loop(0, 4)
-    def _(i):
-        cols = pl.ds(pl.multiple_of(i * 512, 512), 512)
+
+    for i in range(4):
+        cols = pl.ds(i * 512, 512)
         acc[:, cols] = jnp.dot(n_a[...], wo_own[:, cols], preferred_element_type=F32)
+    gain_b[pl.ds(0, NH), :] = gain_ref[pl.ds(g * NH, NH), :]
 
     send_wo.wait_recv()
     for copy in (*send_x, send_wo, send_k, send_q):
@@ -249,16 +262,24 @@
                 remote(tot, tot, s2_sem.at[n, k], q2_sem.at[n, k], partner).wait_send()
 
     prefix_wait(pfb, 1)
-    finish(qkv_r, y_b, pfb, g, n_b)
     span = pl.ds(0, (PLANE - 1) * SL)
     for n in range(2):
         remote(kv_a.at[span], kv_a.at[span], s3_sem.at[n], q3_sem.at[n], partner).wait_send()
 
 
-def out_kernel(acc, n_b, wo_oth, out):
-    cols = pl.ds(pl.multiple_of(pl.program_id(0) * 512, 512), 512)
-    mixed = acc[:, cols] + jnp.dot(n_b[...], wo_oth[:, cols], preferred_element_type=F32)
-    out[0] = mixed.astype(BF16)
+def out_kernel(acc, y_b, qkv_r, pfb, gain_b, wo_oth, out_hbm, n_b, out_v, st_sem):
+    finish(qkv_r, y_b, pfb, gain_b, 0, n_b)
+    copies = []
+    start = 0
+    for n, width in enumerate(WIDTHS):
+        cols = pl.ds(start, width)
+        mixed = acc[:, cols] + jnp.dot(n_b[...], wo_oth[:, cols], preferred_element_type=F32)
+        out_v[:, cols] = mixed.astype(BF16)
+        copies.append(pltpu.make_async_copy(out_v.at[:, cols], out_hbm.at[0, :, cols], st_sem.at[n]))
+        copies[-1].start()
+        start += width
+    for copy in copies:
+        copy.wait()
 
 
 def body(tokens, w_qkv, w_out, gain):
@@ -268,24 +289,27 @@
     dma = pltpu.SemaphoreType.DMA
     scratch = [
         vm((T, D), BF16), vm((T, D), BF16), vm((3, D, HC), BF16), vm((HC, D), BF16), vm((2 * NH, HD), F32),
-        vm((T, 3 * HC), BF16), vm((T, 3 * HC), BF16), vm((T, 3 * HC), BF16),
+        vm((T, 3 * HC), BF16), vm((T, 3 * HC), BF16),
         vm((HC, HD), BF16), vm((HC, HD), BF16),
         vm((PLANE, SL, HD), BF16), vm((PLANE, SL, HD), BF16),
         vm((SL, HD), BF16), vm((SL, HD), BF16),
         vm((NZ, SL, HD), BF16), vm((NZ, SL, HD), BF16),
         vm((PLANE, SL, HD), BF16), vm((PLANE, SL, HD), BF16),
-        vm((HC, HD), BF16), vm((HC, HD), BF16),
-        vm((T, HC), F32), vm((T, HC), F32), vm((T, HC), BF16),
-        dma((6,)), dma((6,)), dma((6,)),
+        vm((HC, HD), BF16), vm((HC, HD), F32),
+        vm((T, HC), F32), vm((T, HC), BF16),
+        dma((7,)), dma((7,)), dma((7,)),
         dma((2,)), dma((2,)), dma((2, NZ)), dma((2, NZ)), dma((2,)), dma((2,)),
         pltpu.SemaphoreType.REGULAR((4,)),
     ]
     whole = pl.BlockSpec(memory_space=pltpu.VMEM)
-    acc, n_b, wo_oth = pl.pallas_call(
+    late = pl.pallas_call(
         kernel,
-        out_shape=[pltpu.VMEM((T, D), F32), pltpu.VMEM((T, HC), BF16), pltpu.VMEM((HC, D), BF16)],
+        out_shape=[
+            vm((T, D), F32), vm((T, HC), F32), vm((T, 3 * HC), BF16), vm((HC, HD), BF16),
+            vm((2 * NH, HD), F32), vm((HC, D), BF16),
+        ],
         in_specs=[any_] * 4,
-        out_specs=[whole, whole, whole],
+        out_specs=[whole] * 6,
         scratch_shapes=scratch,
         compiler_params=pltpu.CompilerParams(
             collective_id=0, has_side_effects=True, vmem_limit_bytes=32 * 1024 * 1024
@@ -295,12 +319,12 @@
     return pl.pallas_call(
         out_kernel,
         out_shape=jax.ShapeDtypeStruct((1, T, D), BF16),
-        grid=(4,),
-        in_specs=[whole, whole, whole],
-        out_specs=pl.BlockSpec((1, T, 512), lambda i: (0, 0, i)),
+        in_specs=[whole] * 6,
+        out_specs=any_,
+        scratch_shapes=[vm((T, HC), BF16), vm((T, D), BF16), dma((len(WIDTHS),))],
         compiler_params=pltpu.CompilerParams(vmem_limit_bytes=16 * 1024 * 1024),
         cost_estimate=pl.CostEstimate(flops=1_000_000_000, bytes_accessed=2_000_000, transcendentals=0),
-    )(acc, n_b, wo_oth)
+    )(*late)
 
 
 def solution(mesh):

time: 28.3 us -> 27.1 us (0.958)
  Pallas kernels: 28.2 us -> 27 us
    pallas_call x1, Pallas kernels: 25.3 us -> 24.5 us  [body(): pl.pallas_call(kernel, out_shape=[vm((T, D), F32), vm((T, HC), F32), vm((...]
    pallas_call x1, Pallas kernels: 2.94 us -> 2.46 us  [body(): pl.pallas_call(out_kernel, out_shape=jax.ShapeDtypeStruct((1, T, D), BF16...]
where the time goes in v4:
time: 27.1 us; the launch traced here: 27 us
  Pallas kernels  27 us (100%)
    pallas_call x1, Pallas kernels, body(): pl.pallas_call(kernel, out_shape=[vm((T, D), F32), vm((T, HC), F32), vm((...  24.5 us
    pallas_call x1, Pallas kernels, body(): pl.pallas_call(out_kernel, out_shape=jax.ShapeDtypeStruct((1, T, D), BF16...  2.46 us

profile of v4, /device:TPU:224, one launch (start us, length us, event | category | flops | bytes accessed | tf_op | source)
XLA Modules:
  0.0 27.0 jit_solution(9322099734092903886)
XLA Ops:
  0.0 24.5 %shard_map.46 = (f32[512,2048]{1,0:T(8,128)S(1)}, f32[512,512]{1,0:T(8,128)S(1)}, bf16[512,1536]{1,0:T(8,128)(2,1)S(1)}, bf16[512,128]{1,0:T(8,128)(2,1)S(1)}, f...) custom-call(bf16[1,512,2048]{2,1,0:T(8,128)(2,1)} %x_hbm.1, bf16[3,2048,512]{2,1,0:T(8,128)(2,1)} %bitcast.2, ...), custom_call_target="tpu_custom_call" | custom-call | flops 8999999488 | bytes 12000000 | tf_op jit(solution)/shard_map/pallas_call | solution.py:305
  24.5 2.5 %shard_map.47 = bf16[1,512,2048]{2,1,0:T(8,128)(2,1)} custom-call(f32[512,2048]{1,0:T(8,128)S(1)} %get-tuple-element.11.acc, f32[512,512]{1,0:T(8,128)S(1)} %get-tuple-element.12.y_b, bf16[512,1536]{1,0:T(8,128)(2,1)S(1)} %get-tuple-element.13.qkv_r, bf16[512,128]{1,0:T(8,128)(2,1)S(1)} %get-tuple-element.14.pfb, f32[8,128]{1,0:T(8,128)S(1)} %get-tuple-element.15.gain_b, ...), custom_call_target="tpu_custom_call" | custom-call | flops 1000000000 | bytes 2000000 | tf_op jit(solution)/shard_map/pallas_call | solution.py:319

commit v5 on v4

--- a/solution.py
+++ b/solution.py
@@ -17,6 +17,7 @@
 BF16 = jnp.bfloat16
 MESH = pl.DeviceIdType.MESH
 WIDTHS = (512, 512, 512, 256, 256)
+SOON = 5
 FAR = sorted(((dx, dy) for dx in range(4) for dy in range(4)), key=lambda o: -min(o[0], 4 - o[0]) - min(o[1], 4 - o[1]))
 
 
@@ -221,22 +222,40 @@
     loads[4].wait()
     project(x_oth, 0, qkv_s)
     send_q.start()
+    scatter_wait(kv_a, r1a, 0, 1)
+
+    @pl.when(z < NZ - 1)
+    def _():
+        pl.semaphore_wait(in_sem.at[3], NZ - 1 - z)
+
+    totals_start(r1a, t2a, r2a, 0)
+    project(x_own, 0, qkv_a)
     send_wo.start()
-    project(x_own, 0, qkv_a)
-    scatter_wait(kv_a, r1a, 0, 1)
-
-    @pl.when(z < NZ - 1)
-    def _():
-        pl.semaphore_wait(in_sem.at[3], NZ - 1 - z)
-
-    totals_start(r1a, t2a, r2a, 0)
-    intra(qkv_a, y_a)
+
+    @pl.when(z < SOON)
+    def _():
+        prefix_start(r1a, t2a, r2a, o3a, pfa, 0)
+
     scatter_wait(kv_b, r1b, 1, 0)
     totals_start(r1b, t2b, r2b, 1)
-    prefix_start(r1a, t2a, r2a, o3a, pfa, 0)
-    prefix_start(r1b, t2b, r2b, o3b, pfb, 1)
+
+    @pl.when(z < SOON)
+    def _():
+        prefix_start(r1b, t2b, r2b, o3b, pfb, 1)
+
+    intra(qkv_a, y_a)
+
+    @pl.when(z >= SOON)
+    def _():
+        prefix_start(r1a, t2a, r2a, o3a, pfa, 0)
+
     send_k.wait_recv()
     send_q.wait_recv()
+
+    @pl.when(z >= SOON)
+    def _():
+        prefix_start(r1b, t2b, r2b, o3b, pfb, 1)
+
     intra(qkv_r, y_b)
     prefix_wait(pfa, 0)
     loads[6].wait()

time: 27.1 us -> 26.3 us (0.970)
  Pallas kernels: 27 us -> 26 us
    pallas_call x1, Pallas kernels: 24.5 us -> 23.6 us  [body(): pl.pallas_call(kernel, out_shape=[vm((T, D), F32), vm((T, HC), F32), vm((...]
where the time goes in v5:
time: 26.3 us; the launch traced here: 26.1 us
  Pallas kernels  26 us (99%)
    pallas_call x1, Pallas kernels, body(): pl.pallas_call(kernel, out_shape=[vm((T, D), F32), vm((T, HC), F32), vm((...  23.6 us
    pallas_call x1, Pallas kernels, body(): pl.pallas_call(out_kernel, out_shape=jax.ShapeDtypeStruct((1, T, D), BF16...  2.46 us

profile of v5, /device:TPU:224, one launch (start us, length us, event | category | flops | bytes accessed | tf_op | source)
XLA Modules:
  0.0 26.1 jit_solution(8144072979120639064)
XLA Ops:
  0.0 23.6 %shard_map.46 = (f32[512,2048]{1,0:T(8,128)S(1)}, f32[512,512]{1,0:T(8,128)S(1)}, bf16[512,1536]{1,0:T(8,128)(2,1)S(1)}, bf16[512,128]{1,0:T(8,128)(2,1)S(1)}, f...) custom-call(bf16[1,512,2048]{2,1,0:T(8,128)(2,1)} %x_hbm.1, bf16[3,2048,512]{2,1,0:T(8,128)(2,1)} %bitcast.2, ...), custom_call_target="tpu_custom_call" | custom-call | flops 8999999488 | bytes 12000000 | tf_op jit(solution)/shard_map/pallas_call | solution.py:324
  23.6 2.5 %shard_map.47 = bf16[1,512,2048]{2,1,0:T(8,128)(2,1)} custom-call(f32[512,2048]{1,0:T(8,128)S(1)} %get-tuple-element.11.acc, f32[512,512]{1,0:T(8,128)S(1)} %get-tuple-element.12.y_b, bf16[512,1536]{1,0:T(8,128)(2,1)S(1)} %get-tuple-element.13.qkv_r, bf16[512,128]{1,0:T(8,128)(2,1)S(1)} %get-tuple-element.14.pfb, f32[8,128]{1,0:T(8,128)S(1)} %get-tuple-element.15.gain_b, ...), custom_call_target="tpu_custom_call" | custom-call | flops 1000000000 | bytes 2000000 | tf_op jit(solution)/shard_map/pallas_call | solution.py:338

commit v6 on v5

--- a/solution.py
+++ b/solution.py
@@ -46,7 +46,7 @@
     acc, y_b, qkv_r, pfb, gain_b, wo_oth,
     x_own, x_oth, w, wo_own, gain_ref,
     qkv_a, qkv_s,
-    kv_a, kv_b, r1a, r1b, t2a, t2b, r2a, r2b, o3a, o3b, pfa, kv_sum,
+    kv_a, kv_b, r1a, r1b, t2a, t2b, r2a, r2b, o3a, o3b, pfa, kv_sum, before,
     y_a, n_a,
     ld_sem, ps_sem, pr_sem, s1_sem, q1_sem, s2_sem, q2_sem, s3_sem, q3_sem, in_sem,
 ):
@@ -76,7 +76,7 @@
         (w_hbm.at[0], w.at[0]), (wo_hbm, wo_own), (gain_hbm, gain_ref),
     )
     loads = [pltpu.make_async_copy(src, dst, ld_sem.at[n]) for n, (src, dst) in enumerate(sources)]
-    for copy in loads[:4]:
+    for copy in loads:
         copy.start()
 
     near = ((1, 0), (3, 0), (0, 1), (0, 3))
@@ -90,7 +90,7 @@
             tell(barrier, f, z + k, p)
 
     partner = (g, c)
-    parts = [pl.ds(0, T // 2), pl.ds(T // 2, T // 4), pl.ds(3 * T // 4, T // 4)]
+    parts = [pl.ds(0, 3 * T // 4), pl.ds(3 * T // 4, T // 4)]
     send_x = [
         remote(x_hbm.at[0, half], x_oth.at[half], ps_sem.at[4 + n], pr_sem.at[4 + n], partner)
         for n, half in enumerate(parts)
@@ -132,7 +132,9 @@
 
     def totals_start(got, tot, r2, n):
         total = got[0].astype(F32)
+        before[n, 0] = jnp.zeros((SL, HD), F32)
         for i in range(1, PLANE):
+            before[n, i] = total
             total = total + got[i].astype(F32)
         tot[...] = total.astype(BF16)
         for k in (4, 3, 5, 2, 6, 1, 7):
@@ -148,14 +150,11 @@
             return total + r2[i].astype(F32)
 
         total = lax.fori_loop(0, z, add, jnp.zeros((SL, HD), F32))
-        for i in range(PLANE):
-            o3[i] = total.astype(BF16)
-            if i < PLANE - 1:
-                total = total + got[i].astype(F32)
         for k in range(PLANE - 1):
             j = chip(k)
+            o3[j] = (total + before[n, j]).astype(BF16)
             remote(o3.at[j], pf.at[rows(p)], s3_sem.at[n], q3_sem.at[n], (f, base + j)).start()
-        pf[rows(p), :] = o3[p]
+        pf[rows(p), :] = (total + before[n, p]).astype(BF16)
 
     def prefix_wait(pf, n):
         m = PLANE - 1
@@ -183,7 +182,7 @@
             y[hi, yc] = jnp.dot(s10, v0, preferred_element_type=F32) + jnp.dot(s11, v1, preferred_element_type=F32)
 
     pl.semaphore_wait(barrier, 5 + z)
-    for copy in (*send_x, *loads[4:]):
+    for copy in send_x:
         copy.start()
     tell(in_sem.at[0], g, z, p)
     for dx, dy in near:
@@ -215,7 +214,7 @@
         copy.wait_recv()
         project(x_oth, 1, qkv_s, part)
         project(x_oth, 2, qkv_s, part)
-        state(qkv_s, kv_b, part, n == 0, n == 2)
+        state(qkv_s, kv_b, part, n == 0, n == 1)
     pl.semaphore_wait(in_sem.at[2], 1)
     scatter_start(kv_b, r1b, g, 1, 0)
     send_k.start()
@@ -314,7 +313,7 @@
         vm((SL, HD), BF16), vm((SL, HD), BF16),
         vm((NZ, SL, HD), BF16), vm((NZ, SL, HD), BF16),
         vm((PLANE, SL, HD), BF16), vm((PLANE, SL, HD), BF16),
-        vm((HC, HD), BF16), vm((HC, HD), F32),
+        vm((HC, HD), BF16), vm((HC, HD), F32), vm((2, PLANE, SL, HD), F32),
         vm((T, HC), F32), vm((T, HC), BF16),
         dma((7,)), dma((7,)), dma((7,)),
         dma((2,)), dma((2,)), dma((2, NZ)), dma((2, NZ)), dma((2,)), dma((2,)),

time: 26.3 us -> 26.2 us (level)
  no operation moved by 1% of the time
where the time goes in v6:
time: 26.2 us; the launch traced here: 26.1 us
  Pallas kernels  26 us (99%)
    pallas_call x1, Pallas kernels, body(): pl.pallas_call(kernel, out_shape=[vm((T, D), F32), vm((T, HC), F32), vm((...  23.6 us
    pallas_call x1, Pallas kernels, body(): pl.pallas_call(out_kernel, out_shape=jax.ShapeDtypeStruct((1, T, D), BF16...  2.46 us

profile of v6, /device:TPU:224, one launch (start us, length us, event | category | flops | bytes accessed | tf_op | source)
XLA Modules:
  0.0 26.1 jit_solution(5372233728017446051)
XLA Ops:
  0.0 23.6 %shard_map.46 = (f32[512,2048]{1,0:T(8,128)S(1)}, f32[512,512]{1,0:T(8,128)S(1)}, bf16[512,1536]{1,0:T(8,128)(2,1)S(1)}, bf16[512,128]{1,0:T(8,128)(2,1)S(1)}, f...) custom-call(bf16[1,512,2048]{2,1,0:T(8,128)(2,1)} %x_hbm.1, bf16[3,2048,512]{2,1,0:T(8,128)(2,1)} %bitcast.2, ...), custom_call_target="tpu_custom_call" | custom-call | flops 8999999488 | bytes 12000000 | tf_op jit(solution)/shard_map/pallas_call | solution.py:323
  23.6 2.5 %shard_map.47 = bf16[1,512,2048]{2,1,0:T(8,128)(2,1)} custom-call(f32[512,2048]{1,0:T(8,128)S(1)} %get-tuple-element.11.acc, f32[512,512]{1,0:T(8,128)S(1)} %get-tuple-element.12.y_b, bf16[512,1536]{1,0:T(8,128)(2,1)S(1)} %get-tuple-element.13.qkv_r, bf16[512,128]{1,0:T(8,128)(2,1)S(1)} %get-tuple-element.14.pfb, f32[8,128]{1,0:T(8,128)S(1)} %get-tuple-element.15.gain_b, ...), custom_call_target="tpu_custom_call" | custom-call | flops 1000000000 | bytes 2000000 | tf_op jit(solution)/shard_map/pallas_call | solution.py:337
